TPU v7x, 256 devices: a whole 4x4x8 slice. The times are simulated.
256 devices in a mesh: ep: 8 (over y, core), seq: 32 (over z, x).
Axes of the slice: x: 4, y: 4, z: 8, core: 2. Of those that a mesh axis runs over, the one named last changes fastest.
Arguments:
- frames: bfloat16 [8, 22528, 512], P('ep', 'seq'), may hold values from -6 to 6
- lengths: int32 [8], P('ep'), may hold values from 11264 to 22528
- w_in: bfloat16 [512, 1024], replicated, may hold values from -0.25 to 0.25
- kernel: float32 [31, 512], replicated, may hold values from -1 to 1
- w_out: bfloat16 [512, 512], replicated, may hold values from -0.25 to 0.25
- pool_query: bfloat16 [8, 512], replicated, may hold values from -600 to 600
- w_value: bfloat16 [512, 512], replicated, may hold values from -0.25 to 0.25
- text_emb: bfloat16 [256, 512], replicated, may hold values from -6 to 6
- teacher: float32 [8, 256], P('ep'), may hold values from -6 to 6
Outputs:
- loss: float32 [], replicated
- grad_in: float32 [512, 1024], P('seq', 'ep')
- grad_out: float32 [512, 512], P('seq', 'ep')
- grad_kernel: float32 [31, 512], replicated
- grad_query: float32 [8, 512], replicated
- grad_value: float32 [512, 512], replicated
All inputs are finite; a program needn't handle non-finite values.
Results may differ from a plain program's by a relative error of at most 0.03.
Values may be sent and summed in bfloat16 or wider, within the bound.
No kernel may reach another device: no remote copies, remote signals or barrier semaphores. Data moves between devices by JAX's collectives and lax.ppermute only.
A program may use at most 64 MiB of HBM per device.

v0:
```python
import jax
import jax.numpy as jnp
from jax import lax
from jax.sharding import PartitionSpec as P


def padded_2(block, sides, width):
    for axis, dim in sides:
        count = lax.axis_size(axis)
        forward = [(i, i + 1) for i in range(count - 1)]
        backward = [(target, source) for source, target in forward]
        low = lax.ppermute(
            lax.slice_in_dim(block, block.shape[dim] - width, None, axis=dim), axis, forward
        )
        high = lax.ppermute(lax.slice_in_dim(block, 0, width, axis=dim), axis, backward)
        block = jnp.concatenate([low, block, high], axis=dim)
    return block


def shards(frames, lengths, w_in, kernel, w_out, pool_query, w_value, text_emb, teacher):
    hi = lax.Precision.HIGHEST
    n_epis, n_rows, width = frames.shape
    n_taps = kernel.shape[0]
    rim = n_taps // 2
    n_heads = pool_query.shape[0]
    head_dim = width // n_heads
    n_cands = text_emb.shape[0]
    root_width = jnp.sqrt(jnp.float32(width))
    offset = lax.axis_index("seq") * n_rows
    positions = offset + jnp.arange(n_rows, dtype=jnp.int32)
    valid = (positions[None, :] < lengths[:, None]).astype(jnp.float32)[..., None]
    xf = frames.astype(jnp.float32)
    mean_val = jnp.mean(xf, axis=-1, keepdims=True)
    var_val = jnp.mean((xf - mean_val) ** 2, axis=-1, keepdims=True)
    normed = ((xf - mean_val) * lax.rsqrt(var_val + 1e-05)).astype(jnp.bfloat16)
    mixed = jnp.einsum("esd,df->esf", normed, w_in, preferred_element_type=jnp.float32)
    sig = jax.nn.sigmoid(mixed[..., width:])
    glu = (mixed[..., :width] * sig * valid).astype(jnp.bfloat16)
    padded = padded_2(glu, (("seq", 1),), rim)
    conv = jnp.zeros((n_epis, n_rows, width), jnp.float32)
    for k in range(n_taps):
        conv = conv + kernel[k] * padded[:, k : k + n_rows].astype(jnp.float32)
    sconv = jax.nn.sigmoid(conv)
    act = (conv * sconv).astype(jnp.bfloat16)
    resid = xf + jnp.einsum("esd,df->esf", act, w_out, preferred_element_type=jnp.float32)
    queries = pool_query.astype(jnp.float32)
    scores = jnp.einsum("esd,hd->esh", resid, queries, precision=hi) / root_width
    masked = jnp.where(valid > 0, scores, -1e30)
    top = lax.pmax(jnp.max(masked, axis=1), "seq")
    expo = jnp.where(valid > 0, jnp.exp(masked - top[:, None]), 0.0)
    vec_here = jnp.einsum("esh,esd->ehd", expo, resid, precision=hi)
    total, vec = lax.psum((jnp.sum(expo, axis=1), vec_here), "seq")
    probs = jnp.where(valid > 0, jnp.exp(masked - top[:, None]), 0.0) / total[:, None]
    vbar = vec / total[..., None]
    wvals = w_value.astype(jnp.float32).reshape(width, n_heads, head_dim)
    pooled = jnp.einsum("ehd,dhk->ehk", vbar, wvals, precision=hi).reshape(n_epis, width)
    rms = jnp.sqrt(jnp.mean(pooled * pooled, axis=-1, keepdims=True) + 1e-06)
    emb = pooled / rms
    texts = text_emb.astype(jnp.float32)
    score = jnp.einsum("ed,cd->ec", emb, texts, precision=hi) / root_width
    diff = score - teacher
    loss_here = jnp.sum(diff * diff) / n_cands
    dscore = 2.0 * diff / n_cands
    demb = jnp.einsum("ec,cd->ed", dscore, texts, precision=hi) / root_width
    dpooled = (demb - emb * jnp.mean(demb * emb, axis=-1, keepdims=True)) / rms
    dp3 = dpooled.reshape(n_epis, n_heads, head_dim)
    value_here = jnp.einsum("ehd,ehk->dhk", vbar, dp3, precision=hi).reshape(width, width)
    dvbar = jnp.einsum("dhk,ehk->ehd", wvals, dp3, precision=hi)
    proj = jnp.einsum("esd,ehd->esh", resid, dvbar, precision=hi)
    centre = jnp.sum(dvbar * vbar, axis=-1)
    dscores = probs * (proj - centre[:, None])
    query_here = jnp.einsum("esh,esd->hd", dscores, resid, precision=hi) / root_width
    dresid = (
        jnp.einsum("esh,ehd->esd", probs, dvbar, precision=hi)
        + jnp.einsum("esh,hd->esd", dscores, queries, precision=hi) / root_width
    ).astype(jnp.bfloat16)
    out_here = jnp.einsum("esd,esf->df", act, dresid, preferred_element_type=jnp.float32)
    dact = jnp.einsum("esf,df->esd", dresid, w_out, preferred_element_type=jnp.float32)
    dconv = (dact * sconv * (1.0 + conv * (1.0 - sconv))).astype(jnp.bfloat16)
    dconv_f = dconv.astype(jnp.float32)
    dpad = padded_2(dconv, (("seq", 1),), rim)
    dglu = jnp.zeros((n_epis, n_rows, width), jnp.float32)
    taps = []
    for k in range(n_taps):
        dglu = dglu + kernel[k] * dpad[:, 2 * rim - k : 2 * rim - k + n_rows].astype(jnp.float32)
        taps.append(jnp.sum(padded[:, k : k + n_rows].astype(jnp.float32) * dconv_f, axis=(0, 1)))
    kernel_here = jnp.stack(taps)
    dglu = dglu * valid
    dmixed = jnp.concatenate(
        [dglu * sig, dglu * mixed[..., :width] * sig * (1.0 - sig)], axis=-1
    ).astype(jnp.bfloat16)
    in_here = jnp.einsum("esd,esf->df", normed, dmixed, preferred_element_type=jnp.float32)
    rows_in, rows_out = (
        lax.psum_scatter(
            in_here.astype(jnp.bfloat16), "seq", scatter_dimension=0, tiled=True
        ).astype(jnp.float32),
        lax.psum_scatter(
            out_here.astype(jnp.bfloat16), "seq", scatter_dimension=0, tiled=True
        ).astype(jnp.float32),
    )
    grad_in, grad_out = (
        lax.psum_scatter(
            rows_in.astype(jnp.bfloat16), "ep", scatter_dimension=1, tiled=True
        ).astype(jnp.float32),
        lax.psum_scatter(
            rows_out.astype(jnp.bfloat16), "ep", scatter_dimension=1, tiled=True
        ).astype(jnp.float32),
    )
    grad_kernel, grad_query = lax.psum((kernel_here, query_here), ("ep", "seq"))
    grad_value, loss = (
        lax.psum(value_here.astype(jnp.bfloat16), "ep").astype(jnp.float32),
        lax.psum(loss_here.astype(jnp.bfloat16), "ep").astype(jnp.float32),
    )
    return (loss, grad_in, grad_out, grad_kernel, grad_query, grad_value)


def solution(mesh):
    return jax.shard_map(
        shards,
        mesh=mesh,
        in_specs=(P("ep", "seq", None), P("ep"), P(), P(), P(), P(), P(), P(), P("ep", None)),
        out_specs=(P(), P("seq", "ep"), P("seq", "ep"), P(), P(), P()),
        check_vma=False,
    )
```

profile of v0, /device:TPU:1, one launch (start us, length us, event | category | flops | bytes accessed | tf_op | source)
XLA Modules:
  0.0 1106.2 jit_solution(10548095060268716896)
XLA Ops:
  8.0 1.3 convert_reduce_fusion
  9.3 1.5 fusion.5
  10.8 0.6 copy-done.88
  11.4 1.0 convolution_bitcast_fusion
  12.8 1.1 copy-done.3
  14.0 3.9 collective-permute-start
  17.9 1.3 collective-permute-start.1
  19.6 1.0 copy.20
  20.6 1.8 collective-permute-done.1
  22.6 9.4 fusion.36
  32.1 0.6 fusion.37
  33.2 0.9 fusion.189
  34.1 62.9 %pmax.7 = f32[8]{0:T(128)S(1)} all-reduce(f32[8]{0:T(128)S(1)} %get-tuple-element.101), channel_id=1, replica_groups=mesh['ep'=8,'seq'=32] {'seq'}, use_global_device_ids=true, to_apply=%region_3.4 | all-reduce | flops 8 | bytes 64 | tf_op jit(solution)/shard_map/pmax | solution.py:49
  97.0 0.7 fusion.164
  97.7 0.8 convolution_bitcast_fusion.3
  98.5 111.0 %all-reduce.1 = (f32[1,8,512]{2,1,0:T(8,128)}, f32[8]{0:T(128)S(1)}) all-reduce(f32[1,8,512]{2,1,0:T(8,128)S(1)} %convolution_bitcast_fusion.3, f32[8]{0:T(128)} %fusion.164), channel_id=1, replica_groups=mesh['ep'=8,'seq'=32] {'seq'}, use_global_device_ids=true, to_apply=%region_4.5 | all-reduce | flops 4104 | bytes 32832 | tf_op jit(solution)/shard_map/psum | solution.py:52
  209.5 0.9 fusion.180
  210.4 1.5 fusion.161
  211.9 0.6 multiply_reduce_fusion
  213.3 0.7 broadcast_divide_fusion.1
  213.9 0.7 div.113
  214.6 0.7 reshape.298
  215.3 1.0 fusion.190
  216.3 0.9 fusion.171
  217.2 1.3 multiply_reduce_fusion.1
  219.1 0.7 subtract_divide_fusion
  219.9 1.4 fusion.191
  221.3 0.9 fusion.181
  222.1 2.1 fusion.159
  224.3 2.0 fusion.94
  226.3 0.8 fusion.93
  227.1 0.5 copy-done.9
  227.7 2.1 fusion.67
  229.9 0.9 copy-done.1
  230.8 1.3 collective-permute-start.2
  232.4 4.2 collective-permute-start.3
  236.5 1.4 convolution_convert_fusion.1
  238.4 25.7 %fusion.96 = (bf16[704,512]{1,0:T(8,128)(2,1)S(1)}, f32[1,704,512]{2,1,0:T(8,128)S(1)}) fusion(f32[1,704,1024]{2,1,0:T(8,128)} %copy-done.3, f32[704]{0:T(1024)S(1)} %copy-done.15, bf16[1,704,512]{2,1,0:T(8,128)(2,1)} %copy-done.1, bf16[1,15,512]{2,1,0:T(8,128)(2,1)S(1)} %collective-permute-done.3, f32[512]{0:T(512)S(1)} %bitcast.173, f32[512]{0:T(512)S(1)} %bitcast.175, ...), kind=kLoop, calls=%fused_computation.235 | loop fusion | flops 67764224 | bytes 4422400 | tf_op jit(solution)/shard_map/concatenate | solution.py:89
  264.1 0.6 fusion.97
  265.2 2.1 convolution_convert_fusion
  267.5 1.0 multiply_convert_fusion.4
  268.5 2.5 fusion.82
  271.1 1.7 fusion.84
  272.8 1.5 fusion.83
  274.3 216.4 %reduce-scatter.11.cloned.1.call-done = bf16[16,512]{1,0:T(8,128)(2,1)} async-done(((bf16[512,512]{1,0:T(8,128)(2,1)}), bf16[16,512]{1,0:T(8,128)(2,1)}) %reduce-scatter.11.cloned.1.call-update) | async-done | bytes 16400 | tf_op jit(solution)/shard_map/reduce_scatter | solution.py:97
  490.6 1.5 copy.28
  492.2 2.2 fusion.68
  494.4 213.8 %reduce-scatter.9.cloned.1.call-done = bf16[16,1024]{1,0:T(8,128)(2,1)} async-done(((bf16[512,1024]{1,0:T(8,128)(2,1)}), bf16[16,1024]{1,0:T(8,128)(2,1)}) %reduce-scatter.9.cloned.1.call-update) | async-done | bytes 32784 | tf_op jit(solution)/shard_map/reduce_scatter | solution.py:94
  708.2 1.6 copy.26
  709.9 1.4 convolution_multiply_fusion.2
  711.3 2.5 stack.127
  713.9 0.6 multiply_reduce_fusion.2
  715.1 18.4 %psum.44 = bf16[]{:T(256)} all-reduce(bf16[]{:T(256)S(6)} %div.117), channel_id=1, replica_groups=mesh['ep'=8,'seq'=32] {'ep'}, use_global_device_ids=true, to_apply=%region_9.10 | all-reduce | flops 1 | bytes 4 | tf_op jit(solution)/shard_map/psum | solution.py:112
  734.2 44.1 %all-reduce.5.cloned.1.call-done = bf16[512,512]{0,1:T(8,128)(2,1)} async-done(((bf16[512,512]{0,1:T(8,128)(2,1)}), bf16[512,512]{0,1:T(8,128)(2,1)}) %all-reduce.5.cloned.1.call-update) | async-done | bytes 524304 | tf_op jit(solution)/shard_map/psum | solution.py:111
  778.2 2.2 copy.21
  780.4 32.0 %reduce-scatter.15.cloned.1.call-done = bf16[64,16]{1,0:T(8,128)(2,1)} async-done(((bf16[512,16]{1,0:T(8,128)(2,1)}), bf16[64,16]{1,0:T(8,128)(2,1)}) %reduce-scatter.15.cloned.1.call-update) | async-done | bytes 2064
  812.4 0.8 copy.29
  813.2 0.6 convert_element_type.365
  813.8 33.0 %reduce-scatter.13.cloned.1.call-done = bf16[128,16]{1,0:T(8,128)(2,1)} async-done(((bf16[1024,16]{1,0:T(8,128)(2,1)}), bf16[128,16]{1,0:T(8,128)(2,1)}) %reduce-scatter.13.cloned.1.call-update) | async-done | bytes 4112
  846.8 0.8 copy.27
  847.6 0.6 convert_element_type.363
  848.3 247.1 %all-reduce.7.cloned.1.call-done = (f32[31,512]{1,0:T(8,128)}, f32[8,512]{1,0:T(8,128)}) async-done(((f32[31,512]{1,0:T(8,128)}, f32[8,512]{1,0:T(8,128)}), (f32[31,512]{1,0:T(8,128)}, f32[8,512]{1,0:T(8,128)})) %all-reduce.7.cloned.1.call-update) | async-done | bytes 79888 | tf_op jit(solution)/shard_map/psum | solution.py:109
  1095.4 1.5 copy.45
  1096.9 1.3 copy.46
  (207 shorter events, 2.5 us)
Async XLA Ops:
  7.2 4.2 copy-start
  7.2 4.2 copy-start.5
  7.2 483.4 %reduce-scatter.11.cloned.1.call-start = ((), (), s32[]{:S(2)}) async-start(), calls=%async_computation.5 | async-start | bytes 540672 | tf_op jit(solution)/shard_map/reduce_scatter | solution.py:97
  12.4 6.8 copy-start.13
  12.4 7.2 copy-start.11
  14.0 6.7 collective-permute-start
  17.9 4.5 collective-permute-start.1
  19.2 3.1 copy-start.18
  19.3 3.1 copy-start.20
  19.3 3.1 copy-start.28
  19.3 3.1 copy-start.30
  19.3 3.1 copy-start.32
  19.3 3.1 copy-start.34
  19.3 3.1 copy-start.36
  19.3 12.7 %copy-start.22 = (f32[1,512]{1,0:T(1,128)}, f32[1,512]{1,0:T(1,128)S(1)}, u32[]{:S(2)}) copy-start(f32[1,512]{1,0:T(1,128)S(1)} %get-tuple-element.89) | copy-start | bytes 6148
  19.3 12.7 %copy-start.24 = (f32[1,512]{1,0:T(1,128)}, f32[1,512]{1,0:T(1,128)S(1)}, u32[]{:S(2)}) copy-start(f32[1,512]{1,0:T(1,128)S(1)} %get-tuple-element.90) | copy-start | bytes 6148
  19.4 12.7 %copy-start.26 = (f32[1,512]{1,0:T(1,128)}, f32[1,512]{1,0:T(1,128)S(1)}, u32[]{:S(2)}) copy-start(f32[1,512]{1,0:T(1,128)S(1)} %get-tuple-element.91) | copy-start | bytes 6148
  20.6 11.5 %copy-start.6 = (bf16[1,704,512]{2,1,0:T(8,128)(2,1)S(1)}, bf16[1,704,512]{2,1,0:T(8,128)(2,1)}, u32[]{:S(2)}) copy-start(bf16[1,704,512]{2,1,0:T(8,128)(2,1)} %param.9) | copy-start | bytes 2162692
  20.6 11.5 %copy-start.90 = (bf16[512,512]{1,0:T(8,128)(2,1)S(1)}, bf16[512,512]{1,0:T(8,128)(2,1)}, u32[]{:S(2)}) copy-start(bf16[512,512]{1,0:T(8,128)(2,1)} %param.13) | copy-start | bytes 1572868
  34.1 181.2 %copy-start.10 = (bf16[256,512]{1,0:T(8,128)(2,1)S(1)}, bf16[256,512]{1,0:T(8,128)(2,1)}, u32[]{:S(2)}) copy-start(bf16[256,512]{1,0:T(8,128)(2,1)} %param.16) | copy-start | bytes 786436
  209.5 11.7 %copy-start.12 = (f32[1,8,512]{2,1,0:T(8,128)S(1)}, f32[1,8,512]{2,1,0:T(8,128)}, u32[]{:S(2)}) copy-start(f32[1,8,512]{2,1,0:T(8,128)} %get-tuple-element.60) | copy-start | bytes 49156
  222.1 4.1 copy-start.17
  230.8 7.3 collective-permute-start.2
  232.0 6.0 copy-start.15
  232.1 6.0 copy-start.19
  232.1 6.0 copy-start.21
  232.1 6.0 copy-start.23
  232.1 6.0 copy-start.25
  232.1 6.0 copy-start.27
  232.1 6.0 copy-start.29
  232.1 6.0 copy-start.31
  232.1 6.0 copy-start.33
  232.1 6.0 copy-start.35
  232.1 6.0 copy-start.37
  232.2 6.0 copy-start.39
  232.2 6.0 copy-start.41
  232.2 6.0 copy-start.43
  232.2 6.0 copy-start.45
  232.2 6.0 copy-start.47
  232.2 6.0 copy-start.49
  232.2 6.0 copy-start.51
  232.2 6.0 copy-start.53
  232.2 6.0 copy-start.55
  232.2 6.0 copy-start.57
  232.3 6.0 copy-start.59
  232.3 6.0 copy-start.61
  232.3 6.0 copy-start.63
  232.3 6.0 copy-start.65
  232.3 6.0 copy-start.67
  232.3 6.0 copy-start.69
  232.3 6.0 copy-start.71
  232.3 6.0 copy-start.73
  232.3 6.0 copy-start.75
  232.3 6.0 copy-start.77
  232.4 6.0 copy-start.79
  232.4 5.7 collective-permute-start.3
  238.0 470.2 %reduce-scatter.9.cloned.1.call-start = ((), (), s32[]{:S(2)}) async-start(), calls=%async_computation.4 | async-start | bytes 1081344 | tf_op jit(solution)/shard_map/reduce_scatter | solution.py:94
  238.1 26.0 %copy-start.4 = (f32[1,704,1024]{2,1,0:T(8,128)S(1)}, f32[1,704,1024]{2,1,0:T(8,128)}, u32[]{:S(2)}) copy-start(f32[1,704,1024]{2,1,0:T(8,128)} %copy-done.3) | copy-start | bytes 8650756
  267.4 510.9 %all-reduce.5.cloned.1.call-start = ((), (), s32[]{:S(2)}) async-start(), calls=%async_computation.6 | async-start | bytes 1048576 | tf_op jit(solution)/shard_map/psum | solution.py:111
  268.5 544.0 %reduce-scatter.15.cloned.1.call-start = ((), (), s32[]{:S(2)}) async-start(), calls=%async_computation.8 | async-start | bytes 147456
  492.1 354.7 %reduce-scatter.13.cloned.1.call-start = ((), (), s32[]{:S(2)}) async-start(), calls=%async_computation.7 | async-start | bytes 294912
  494.4 219.4 %copy-start.84 = (f32[256]{0:T(256)S(1)}, f32[256]{0:T(256)}, u32[]{:S(2)}) copy-start(f32[256]{0:T(256)} %copy-done.83) | copy-start | bytes 3076
  494.4 219.4 %copy-start.87 = (f32[1,256]{1,0:T(1,128)S(1)}, f32[1,256]{1,0:T(1,128)}, u32[]{:S(2)}) copy-start(f32[1,256]{1,0:T(1,128)} %param.17) | copy-start | bytes 3076
  709.8 385.6 %all-reduce.7.cloned.1.call-start = ((), (), s32[]{:S(2)}) async-start(), calls=%async_computation.9 | async-start | bytes 163840 | tf_op jit(solution)/shard_map/psum | solution.py:109
  (38 other events, 84.5 us)
Sparse Core Ops, SparseCore 0:
  238.1 252.4 reduce-scatter.10
  495.5 212.6 reduce-scatter.8
  710.6 67.5 all-reduce.4
  780.6 31.8 reduce-scatter.14
  814.9 31.8 reduce-scatter.12
  852.8 242.5 all-reduce.6
where the time goes:
time: 1110 us
  waiting for transfers between devices  788 us (71%)
  blocking collectives  192 us (17%)
  other arithmetic  55.3 us (5%)
  between operations  20.1 us (2%)
  matrix products  20 us (2%)
  local copies, waits for them, and re-layouts  19.4 us (2%)
    psum x1, waiting for transfers between devices, shards(): grad_kernel, grad_query = lax.psum((kernel_here, query_here), ('ep', 'seq'))  247 us
    reduce_scatter x1, waiting for transfers between devices, shards(): lax.psum_scatter(out_here.astype(jnp.bfloat16), 'seq', scatter_dimension=...  216 us
    reduce_scatter x1, waiting for transfers between devices, shards(): lax.psum_scatter(in_here.astype(jnp.bfloat16), 'seq', scatter_dimension=0...  214 us
    psum x1, blocking collectives, shards(): total, vec = lax.psum((jnp.sum(expo, axis=1), vec_here), 'seq')  111 us
    unnamed x8, waiting for transfers between devices  65.1 us
    pmax x1, blocking collectives, shards(): top = lax.pmax(jnp.max(masked, axis=1), 'seq')  62.9 us
    psum x1, waiting for transfers between devices, shards(): lax.psum(value_here.astype(jnp.bfloat16), 'ep').astype(jnp.float32)  44.1 us
    concatenate x2, other arithmetic, shards(): jnp.concatenate([dglu * sig, dglu * mixed[..., :width] * sig * (1.0 - sig...  26.3 us
  transfers between devices with their start and end apart: 10, of which 7 were waited for; matrix products, arithmetic and copies ran while one was open for 5% of the time, Pallas kernels for 0%

commit v1 on v0

--- a/solution.py
+++ b/solution.py
@@ -1,7 +1,15 @@
+import functools
 import jax
 import jax.numpy as jnp
 from jax import lax
 from jax.sharding import PartitionSpec as P
+
+
+def form_vectors(array_in, bus_axis, across):
+    return lax.psum(lax.psum(array_in, axis_name=bus_axis), axis_name=across)
+
+
+replace_boxes = functools.partial(form_vectors, bus_axis="ep", across="seq")
 
 
 def padded_2(block, sides, width):
@@ -106,7 +114,7 @@
             rows_out.astype(jnp.bfloat16), "ep", scatter_dimension=1, tiled=True
         ).astype(jnp.float32),
     )
-    grad_kernel, grad_query = lax.psum((kernel_here, query_here), ("ep", "seq"))
+    grad_kernel, grad_query = replace_boxes((kernel_here, query_here))
     grad_value, loss = (
         lax.psum(value_here.astype(jnp.bfloat16), "ep").astype(jnp.float32),
         lax.psum(loss_here.astype(jnp.bfloat16), "ep").astype(jnp.float32),

time: 1110 us -> 871 us (0.78)
  waiting for transfers between devices: 788 us -> 548 us
    psum x1 -> x2, waiting for transfers between devices: 247 us -> 72.7 us  [form_vectors(): return lax.psum(lax.psum(array_in, axis_name=bus_axis), axis_name=across)]
    psum x1, waiting for transfers between devices: 44.1 us -> 0.03 us  [shards(): lax.psum(value_here.astype(jnp.bfloat16), 'ep').astype(jnp.float32)]
    unnamed x8 -> x9, waiting for transfers between devices: 65.1 us -> 45.9 us
  transfers between devices with their start and end apart: 10 -> 11, of which waited for: 7 -> 6; matrix products, arithmetic and copies ran while one was open for 5% -> 6% of each run, Pallas kernels for 0% -> 0%
where the time goes in v1:
time: 871 us; the launch traced here: 866 us
  waiting for transfers between devices  548 us (63%)
  blocking collectives  192 us (22%)
  other arithmetic  54.3 us (6%)
  between operations  21.5 us (2%)
  matrix products  20 us (2%)
  local copies, waits for them, and re-layouts  19.4 us (2%)
  starting transfers between devices  11 us (1%)
    reduce_scatter x1, waiting for transfers between devices, shards(): lax.psum_scatter(in_here.astype(jnp.bfloat16), 'seq', scatter_dimension=0...  216 us
    reduce_scatter x1, waiting for transfers between devices, shards(): lax.psum_scatter(out_here.astype(jnp.bfloat16), 'seq', scatter_dimension=...  211 us
    psum x1, blocking collectives, shards(): total, vec = lax.psum((jnp.sum(expo, axis=1), vec_here), 'seq')  111 us
    psum x2, waiting for transfers between devices, form_vectors(): return lax.psum(lax.psum(array_in, axis_name=bus_axis), axis_name=across)  72.7 us
    pmax x1, blocking collectives, shards(): top = lax.pmax(jnp.max(masked, axis=1), 'seq')  62.9 us
    unnamed x9, waiting for transfers between devices  45.9 us
    concatenate x2, other arithmetic, shards(): jnp.concatenate([dglu * sig, dglu * mixed[..., :width] * sig * (1.0 - sig...  26.3 us
    psum x1, blocking collectives, shards(): lax.psum(loss_here.astype(jnp.bfloat16), 'ep').astype(jnp.float32)  18.1 us
  transfers between devices with their start and end apart: 11, of which 6 were waited for; matrix products, arithmetic and copies ran while one was open for 6% of the time, Pallas kernels for 0%

profile of v1, /device:TPU:1, one launch (start us, length us, event | category | flops | bytes accessed | tf_op | source)
XLA Modules:
  0.0 866.0 jit_solution(17126749846028417517)
XLA Ops:
  8.8 1.3 convert_reduce_fusion
  10.2 1.5 fusion.5
  11.7 0.6 copy-done.88
  12.2 1.0 convolution_bitcast_fusion
  13.7 1.1 copy-done.3
  14.8 3.9 collective-permute-start
  18.7 1.3 collective-permute-start.1
  20.5 1.0 copy.20
  21.5 1.8 collective-permute-done.1
  23.5 9.4 %fusion.36 = f32[1,704,512]{2,1,0:T(8,128)S(1)} fusion(bf16[1,704,512]{2,1,0:T(8,128)(2,1)S(1)} %multiply_convert_fusion.3, bf16[1,15,512]{2,1,0:T(8,128)(2,1)S(1)} %collective-permute-done.1, bf16[1,15,512]{2,1,0:T(8,128)(2,1)S(1)} %collective-permute-done, f32[512]{0:T(512)S(1)} %bitcast.172, f32[512]{0:T(512)S(1)} %bitcast.174, f32[512]{0:T(512)S(1)} %bitcast.178, ...), kind=kLoop, calls=%fused_computation.163 | loop fusion | flops 65601536 | bytes 2256896 | tf_op jit(solution)/shard_map/add | solution.py:50
  33.0 0.6 fusion.37
  33.5 0.5 copy-done.8
  34.1 0.9 fusion.189
  34.9 62.9 %pmax.7 = f32[8]{0:T(128)S(1)} all-reduce(f32[8]{0:T(128)S(1)} %get-tuple-element.103), channel_id=1, replica_groups=mesh['ep'=8,'seq'=32] {'seq'}, use_global_device_ids=true, to_apply=%region_3.4 | all-reduce | flops 8 | bytes 64 | tf_op jit(solution)/shard_map/pmax | solution.py:57
  97.8 0.7 fusion.164
  98.5 0.8 convolution_bitcast_fusion.3
  99.3 111.0 %all-reduce.1 = (f32[1,8,512]{2,1,0:T(8,128)}, f32[8]{0:T(128)S(1)}) all-reduce(f32[1,8,512]{2,1,0:T(8,128)S(1)} %convolution_bitcast_fusion.3, f32[8]{0:T(128)} %fusion.164), channel_id=1, replica_groups=mesh['ep'=8,'seq'=32] {'seq'}, use_global_device_ids=true, to_apply=%region_4.5 | all-reduce | flops 4104 | bytes 32832 | tf_op jit(solution)/shard_map/psum | solution.py:60
  210.3 0.9 fusion.180
  211.2 1.5 fusion.161
  212.8 0.6 multiply_reduce_fusion
  214.1 0.7 broadcast_divide_fusion.1
  214.8 0.7 div.113
  215.5 0.7 reshape.298
  216.1 1.0 fusion.190
  217.1 0.9 fusion.171
  218.0 1.3 multiply_reduce_fusion.1
  220.0 0.7 subtract_divide_fusion
  220.7 1.4 fusion.191
  222.1 0.9 fusion.181
  223.0 2.1 fusion.159
  225.1 2.0 fusion.94
  227.1 0.8 fusion.93
  227.9 0.5 copy-done.9
  228.6 2.2 fusion.67
  230.7 0.9 copy-done.1
  231.6 1.3 collective-permute-start.2
  233.2 4.2 collective-permute-start.3
  237.4 1.4 convolution_convert_fusion.1
  239.3 25.7 %fusion.96 = (bf16[704,512]{1,0:T(8,128)(2,1)S(1)}, f32[1,704,512]{2,1,0:T(8,128)S(1)}) fusion(f32[1,704,1024]{2,1,0:T(8,128)} %copy-done.3, f32[704]{0:T(1024)S(1)} %copy-done.15, bf16[1,704,512]{2,1,0:T(8,128)(2,1)} %copy-done.1, bf16[1,15,512]{2,1,0:T(8,128)(2,1)S(1)} %collective-permute-done.3, f32[512]{0:T(512)S(1)} %bitcast.173, f32[512]{0:T(512)S(1)} %bitcast.175, ...), kind=kLoop, calls=%fused_computation.235 | loop fusion | flops 67764224 | bytes 4422400 | tf_op jit(solution)/shard_map/concatenate | solution.py:97
  265.1 0.6 fusion.97
  266.1 2.1 convolution_convert_fusion
  268.4 2.3 fusion.68
  270.7 1.5 fusion.82
  272.1 1.5 fusion.83
  273.6 1.7 fusion.84
  275.3 2.5 stack.127
  277.9 1.4 convolution_multiply_fusion.2
  279.4 0.9 multiply_convert_fusion.4
  280.4 211.1 %reduce-scatter.11.cloned.1.call-done = bf16[16,512]{1,0:T(8,128)(2,1)} async-done(((bf16[512,512]{1,0:T(8,128)(2,1)}), bf16[16,512]{1,0:T(8,128)(2,1)}) %reduce-scatter.11.cloned.1.call-update) | async-done | bytes 16400 | tf_op jit(solution)/shard_map/reduce_scatter | solution.py:105
  491.5 1.5 copy.28
  493.0 216.3 %reduce-scatter.9.cloned.1.call-done = bf16[16,1024]{1,0:T(8,128)(2,1)} async-done(((bf16[512,1024]{1,0:T(8,128)(2,1)}), bf16[16,1024]{1,0:T(8,128)(2,1)}) %reduce-scatter.9.cloned.1.call-update) | async-done | bytes 32784 | tf_op jit(solution)/shard_map/reduce_scatter | solution.py:102
  709.3 1.6 copy.26
  711.5 0.6 multiply_reduce_fusion.2
  712.8 18.1 %psum.58 = bf16[]{:T(256)} all-reduce(bf16[]{:T(256)S(6)} %div.117), channel_id=1, replica_groups=mesh['ep'=8,'seq'=32] {'ep'}, use_global_device_ids=true, to_apply=%region_9.10 | all-reduce | flops 1 | bytes 4 | tf_op jit(solution)/shard_map/psum | solution.py:120
  731.6 2.2 copy.21
  733.9 12.5 %reduce-scatter.15.cloned.1.call-done = bf16[64,16]{1,0:T(8,128)(2,1)} async-done(((bf16[512,16]{1,0:T(8,128)(2,1)}), bf16[64,16]{1,0:T(8,128)(2,1)}) %reduce-scatter.15.cloned.1.call-update) | async-done | bytes 2064
  746.3 0.8 copy.29
  747.1 0.6 convert_element_type.365
  747.7 32.9 %reduce-scatter.13.cloned.1.call-done = bf16[128,16]{1,0:T(8,128)(2,1)} async-done(((bf16[1024,16]{1,0:T(8,128)(2,1)}), bf16[128,16]{1,0:T(8,128)(2,1)}) %reduce-scatter.13.cloned.1.call-update) | async-done | bytes 4112
  780.6 0.8 copy.27
  781.4 0.6 convert_element_type.363
  782.1 72.6 %all-reduce.9.cloned.1.call-done = (f32[31,512]{1,0:T(8,128)}, f32[8,512]{1,0:T(8,128)}) async-done(((f32[31,512]{1,0:T(8,128)}, f32[8,512]{1,0:T(8,128)}), (f32[31,512]{1,0:T(8,128)}, f32[8,512]{1,0:T(8,128)})) %all-reduce.9.cloned.1.call-update) | async-done | bytes 79888 | tf_op jit(solution)/shard_map/psum | solution.py:9
  854.7 1.5 copy.47
  856.2 1.3 copy.48
  (210 shorter events, 2.6 us)
Async XLA Ops:
  8.0 4.2 copy-start
  8.0 4.2 copy-start.5
  8.0 483.5 %reduce-scatter.11.cloned.1.call-start = ((), (), s32[]{:S(2)}) async-start(), calls=%async_computation.5 | async-start | bytes 540672 | tf_op jit(solution)/shard_map/reduce_scatter | solution.py:105
  13.2 6.8 copy-start.13
  13.2 7.2 copy-start.11
  14.8 6.7 collective-permute-start
  18.7 4.5 collective-permute-start.1
  20.1 3.1 copy-start.18
  20.1 3.1 copy-start.20
  20.1 3.1 copy-start.28
  20.1 3.1 copy-start.30
  20.1 3.1 copy-start.32
  20.1 3.1 copy-start.34
  20.2 12.7 %copy-start.22 = (f32[1,512]{1,0:T(1,128)}, f32[1,512]{1,0:T(1,128)S(1)}, u32[]{:S(2)}) copy-start(f32[1,512]{1,0:T(1,128)S(1)} %get-tuple-element.91) | copy-start | bytes 6148
  20.2 12.7 %copy-start.24 = (f32[1,512]{1,0:T(1,128)}, f32[1,512]{1,0:T(1,128)S(1)}, u32[]{:S(2)}) copy-start(f32[1,512]{1,0:T(1,128)S(1)} %get-tuple-element.92) | copy-start | bytes 6148
  20.2 12.7 %copy-start.26 = (f32[1,512]{1,0:T(1,128)}, f32[1,512]{1,0:T(1,128)S(1)}, u32[]{:S(2)}) copy-start(f32[1,512]{1,0:T(1,128)S(1)} %get-tuple-element.93) | copy-start | bytes 6148
  21.5 11.5 %copy-start.6 = (bf16[1,704,512]{2,1,0:T(8,128)(2,1)S(1)}, bf16[1,704,512]{2,1,0:T(8,128)(2,1)}, u32[]{:S(2)}) copy-start(bf16[1,704,512]{2,1,0:T(8,128)(2,1)} %param.9) | copy-start | bytes 2162692
  21.5 11.5 %copy-start.90 = (bf16[512,512]{1,0:T(8,128)(2,1)S(1)}, bf16[512,512]{1,0:T(8,128)(2,1)}, u32[]{:S(2)}) copy-start(bf16[512,512]{1,0:T(8,128)(2,1)} %param.13) | copy-start | bytes 1572868
  34.9 181.2 %copy-start.10 = (bf16[256,512]{1,0:T(8,128)(2,1)S(1)}, bf16[256,512]{1,0:T(8,128)(2,1)}, u32[]{:S(2)}) copy-start(bf16[256,512]{1,0:T(8,128)(2,1)} %param.16) | copy-start | bytes 786436
  210.3 11.7 %copy-start.12 = (f32[1,8,512]{2,1,0:T(8,128)S(1)}, f32[1,8,512]{2,1,0:T(8,128)}, u32[]{:S(2)}) copy-start(f32[1,8,512]{2,1,0:T(8,128)} %get-tuple-element.60) | copy-start | bytes 49156
  223.0 4.1 copy-start.17
  231.6 7.4 collective-permute-start.2
  232.9 6.1 copy-start.15
  232.9 6.1 copy-start.19
  232.9 6.1 copy-start.21
  232.9 6.1 copy-start.23
  232.9 6.1 copy-start.25
  232.9 6.1 copy-start.27
  232.9 6.1 copy-start.29
  233.0 6.1 copy-start.31
  233.0 6.1 copy-start.33
  233.0 6.1 copy-start.35
  233.0 6.1 copy-start.37
  233.0 6.1 copy-start.39
  233.0 6.1 copy-start.41
  233.0 6.1 copy-start.43
  233.0 6.1 copy-start.45
  233.0 6.1 copy-start.47
  233.0 6.1 copy-start.49
  233.1 6.1 copy-start.51
  233.1 6.1 copy-start.53
  233.1 6.1 copy-start.55
  233.1 6.1 copy-start.57
  233.1 6.1 copy-start.59
  233.1 6.1 copy-start.61
  233.1 6.1 copy-start.63
  233.1 6.1 copy-start.65
  233.1 6.1 copy-start.67
  233.1 6.1 copy-start.69
  233.2 6.1 copy-start.71
  233.2 6.1 copy-start.73
  233.2 6.1 copy-start.75
  233.2 6.1 copy-start.77
  233.2 6.1 copy-start.79
  233.2 5.8 collective-permute-start.3
  238.9 470.4 %reduce-scatter.9.cloned.1.call-start = ((), (), s32[]{:S(2)}) async-start(), calls=%async_computation.4 | async-start | bytes 1081344 | tf_op jit(solution)/shard_map/reduce_scatter | solution.py:102
  239.0 26.0 %copy-start.4 = (f32[1,704,1024]{2,1,0:T(8,128)S(1)}, f32[1,704,1024]{2,1,0:T(8,128)}, u32[]{:S(2)}) copy-start(f32[1,704,1024]{2,1,0:T(8,128)} %copy-done.3) | copy-start | bytes 8650756
  268.3 442.7 %all-reduce.11.cloned.1.call-start = ((), (), s32[]{:S(2)}) async-start(), calls=%async_computation.10 | async-start | bytes 163840 | tf_op jit(solution)/shard_map/psum | solution.py:9
  277.9 433.6 %copy-start.84 = (f32[256]{0:T(256)S(1)}, f32[256]{0:T(256)}, u32[]{:S(2)}) copy-start(f32[256]{0:T(256)} %copy-done.83) | copy-start | bytes 3076
  277.9 433.7 %copy-start.87 = (f32[1,256]{1,0:T(1,128)S(1)}, f32[1,256]{1,0:T(1,128)}, u32[]{:S(2)}) copy-start(f32[1,256]{1,0:T(1,128)} %param.17) | copy-start | bytes 3076
  279.3 452.3 %all-reduce.7.cloned.1.call-start = ((), (), s32[]{:S(2)}) async-start(), calls=%async_computation.6 | async-start | bytes 1048576 | tf_op jit(solution)/shard_map/psum | solution.py:119
  280.3 466.0 %reduce-scatter.15.cloned.1.call-start = ((), (), s32[]{:S(2)}) async-start(), calls=%async_computation.8 | async-start | bytes 147456
  493.0 287.6 %reduce-scatter.13.cloned.1.call-start = ((), (), s32[]{:S(2)}) async-start(), calls=%async_computation.7 | async-start | bytes 294912
  710.9 143.8 %all-reduce.9.cloned.1.call-start = ((), (), s32[]{:S(2)}) async-start(), calls=%async_computation.9 | async-start | bytes 163840 | tf_op jit(solution)/shard_map/psum | solution.py:9
  (39 other events, 87.4 us)
Sparse Core Ops, SparseCore 0:
  239.0 252.4 reduce-scatter.10
  496.4 212.8 reduce-scatter.8
  712.0 34.3 reduce-scatter.14
  748.7 31.9 reduce-scatter.12
Sparse Core Ops, SparseCore 1:
  279.4 108.4 all-reduce.10
  390.1 63.9 all-reduce.6
  715.3 139.3 all-reduce.8
